TPU v7x, 32 devices: a whole 2x2x4 slice. The times are simulated.
32 devices in a mesh: section: 4 (over y, x), dp: 2 (over core), mp: 4 (over z).
Axes of the slice: x: 2, y: 2, z: 4, core: 2. Of those that a mesh axis runs over, the one named last changes fastest.
Arguments:
- enc_hidden: bfloat16 [2, 128, 4096], P('dp', None, ('section', 'mp')), may hold values from -32 to 32
- enc_gain: float32 [4096], replicated, may hold values from 0.1 to 1.9
- key_weight: bfloat16 [4, 4096, 2048], P('section', None, 'mp'), may hold values from -0.09375 to 0.09375
- value_weight: bfloat16 [4, 4096, 2048], P('section', None, 'mp'), may hold values from -0.25 to 0.25
- queries: bfloat16 [2, 4, 256, 2048], P('dp', 'section', None, 'mp'), may hold values from -256 to 256
- out_grad: bfloat16 [2, 4, 256, 2048], P('dp', 'section', None, 'mp'), may hold values from -4 to 4
Outputs:
- attended: bfloat16 [2, 4, 256, 2048], P('dp', 'section', None, 'mp')
- query_grad: bfloat16 [2, 4, 256, 2048], P('dp', 'section', None, 'mp')
- hidden_grad: float32 [2, 128, 4096], P('dp', None, ('section', 'mp'))
- gain_grad: float32 [4096], P(('section', 'mp'))
All inputs are finite; a program needn't handle non-finite values.
Results may differ from a plain program's by a relative error of at most 0.02.
The roundings to bfloat16 on the way count: a program that leaves them out, or rounds other values in their place, can miss the bound.
Values may be sent and summed in bfloat16 or wider, within the bound.
No kernel may reach another device: no remote copies, remote signals or barrier semaphores. Data moves between devices by JAX's collectives and lax.ppermute only.
A program may use at most 64 MiB of HBM per device.

v0:
```python
import jax
import jax.numpy as jnp
from jax import lax
from jax.sharding import PartitionSpec as P

DH = 64
epsilon = 1e-06


def attend(key_value, queries, out_grad, columns):
    batch, source_length, _ = key_value.shape
    head_count = columns // DH
    factor = DH ** (-0.5)
    keys = key_value[..., :columns].reshape(batch, source_length, head_count, DH)
    values = key_value[..., columns:].reshape(batch, source_length, head_count, DH)
    asked = queries[:, 0].reshape(batch, -1, head_count, DH)
    upstream = out_grad[:, 0].reshape(batch, -1, head_count, DH)
    target_length = asked.shape[1]
    scores = jnp.einsum("sqhd,skhd->shqk", asked, keys, preferred_element_type=jnp.float32) * factor
    highest = jnp.max(scores, axis=-1, keepdims=True)
    raised = jnp.exp(scores - highest)
    shares = raised / jnp.sum(raised, axis=-1, keepdims=True)
    shares_low = shares.astype(jnp.bfloat16)
    attended = jnp.einsum(
        "shqk,skhd->sqhd", shares_low, values, preferred_element_type=jnp.float32
    ).astype(jnp.bfloat16)
    share_grad = jnp.einsum("sqhd,skhd->shqk", upstream, values, preferred_element_type=jnp.float32)
    value_grad = jnp.einsum(
        "shqk,sqhd->skhd", shares_low, upstream, preferred_element_type=jnp.float32
    ).astype(jnp.bfloat16)
    score_grad = (
        shares * (share_grad - jnp.sum(shares * share_grad, axis=-1, keepdims=True)) * factor
    )
    score_low = score_grad.astype(jnp.bfloat16)
    query_grad = jnp.einsum(
        "shqk,skhd->sqhd", score_low, keys, preferred_element_type=jnp.float32
    ).astype(jnp.bfloat16)
    key_grad = jnp.einsum(
        "shqk,sqhd->skhd", score_low, asked, preferred_element_type=jnp.float32
    ).astype(jnp.bfloat16)
    return (
        attended.reshape(batch, 1, target_length, columns),
        query_grad.reshape(batch, 1, target_length, columns),
        key_grad.reshape(batch, source_length, columns),
        value_grad.reshape(batch, source_length, columns),
    )


def per_device(enc_hidden, enc_gain, key_weight, value_weight, queries, out_grad):
    batch, source_length, own_columns = enc_hidden.shape
    width = key_weight.shape[1]
    columns = key_weight.shape[2]
    key_matrix = key_weight[0]
    value_matrix = value_weight[0]
    replicas = batch * lax.axis_size("dp")
    sections = lax.axis_size("section")
    groups = lax.axis_size("mp")
    first_column = lax.axis_index(("section", "mp")) * own_columns
    gain_own = lax.dynamic_slice_in_dim(enc_gain, first_column, own_columns, 0)
    widened = enc_hidden.astype(jnp.float32)
    squares = lax.psum(jnp.sum(widened * widened, axis=-1, keepdims=True), ("section", "mp"))
    inverse = lax.rsqrt(squares / width + epsilon)
    normed = widened * inverse
    own_memory = (normed * gain_own).astype(jnp.bfloat16)
    memory = lax.all_gather(own_memory, ("section", "mp"), axis=2, tiled=True)
    flat = memory.reshape(-1, width)
    keys = jnp.dot(flat, key_matrix, preferred_element_type=jnp.float32).astype(jnp.bfloat16)
    values = jnp.dot(flat, value_matrix, preferred_element_type=jnp.float32).astype(jnp.bfloat16)
    key_value = jnp.concatenate((keys, values), axis=-1).reshape(batch, source_length, 2 * columns)
    attended, query_grad, key_grad, value_grad = attend(key_value, queries, out_grad, columns)
    total = jnp.einsum("skc,dc->skd", key_grad, key_matrix, preferred_element_type=jnp.float32)
    head_part = (
        total
        + jnp.einsum("skc,dc->skd", value_grad, value_matrix, preferred_element_type=jnp.float32)
    ).reshape(batch, source_length, sections, groups, own_columns)
    layer_part = lax.psum_scatter(
        head_part.astype(jnp.bfloat16), "mp", scatter_dimension=3, tiled=True
    )
    own_grad = (
        lax.psum_scatter(layer_part, "section", scatter_dimension=2, tiled=True)
        .astype(jnp.float32)
        .reshape(batch, source_length, own_columns)
    )
    scaled = own_grad * gain_own
    mean_total = lax.psum(jnp.sum(scaled * normed, axis=-1, keepdims=True), ("section", "mp"))
    gain_total = lax.psum(jnp.sum(own_grad * normed, axis=(0, 1)), "dp")
    hidden_grad = inverse * (scaled - normed * (mean_total / width))
    gain_grad = gain_total / replicas
    return (attended, query_grad, hidden_grad, gain_grad)


def solution(mesh):
    in_specs = (
        P("dp", None, ("section", "mp")),
        P(),
        P("section", None, "mp"),
        P("section", None, "mp"),
        P("dp", "section", None, "mp"),
        P("dp", "section", None, "mp"),
    )
    out_specs = (
        P("dp", "section", None, "mp"),
        P("dp", "section", None, "mp"),
        P("dp", None, ("section", "mp")),
        P(("section", "mp")),
    )
    return jax.shard_map(
        per_device, mesh=mesh, in_specs=in_specs, out_specs=out_specs, check_vma=False
    )
```

profile of v0, /device:TPU:0, one launch (start us, length us, event | category | flops | bytes accessed | tf_op | source)
XLA Modules:
  0.0 253.4 jit_solution(6738457621057778831)
XLA Ops:
  7.2 0.9 fusion.40
  8.2 43.7 %psum.21 = f32[1,128,1]{1,2,0:T(1,128)S(1)} all-reduce(f32[1,128,1]{1,2,0:T(1,128)S(1)} %bitcast.127), channel_id=1, replica_groups=mesh['section'=4,'dp'=2,'mp'=4] {'section','mp'}, use_global_device_ids=true, to_apply=%region_1.0 | all-reduce | flops 128 | bytes 1024 | tf_op jit(solution)/shard_map/psum | solution.py:61
  52.7 1.6 fusion.38
  54.3 1.1 copy.38
  55.4 1.1 copy.40
  56.5 49.2 %all-gather.2.cloned.1.call-done = bf16[1,128,4096]{2,1,0:T(8,128)(2,1)} async-done(((bf16[1,128,256]{2,1,0:T(8,128)(2,1)}), bf16[1,128,4096]{2,1,0:T(8,128)(2,1)}) %all-gather.2.cloned.1.call-update) | async-done | bytes 1048592 | tf_op jit(solution)/shard_map/all_gather | solution.py:65
  105.7 3.4 %fusion.20 = bf16[128,512]{1,0:T(8,128)(2,1)S(1)} fusion(bf16[1,4096,512]{2,1,0:T(8,128)(2,1)} %param.9, bf16[1,128,4096]{2,1,0:T(8,128)(2,1)} %all-gather.2.cloned.1.call-done), kind=kOutput, calls=%fused_computation.23 | convolution fusion | flops 536936448 | bytes 5373952 | tf_op jit(solution)/shard_map/dot_general | solution.py:68
  110.8 1.5 fusion.49
  113.4 2.0 convolution_convert_fusion.3
  115.4 3.8 %fusion.6 = f32[128,4096]{1,0:T(8,128)S(1)} fusion(bf16[128,512]{0,1:T(8,128)(2,1)S(1)} %bitcast.121, bf16[1,4096,512]{2,1,0:T(8,128)(2,1)} %param.8), kind=kOutput, calls=%fused_computation.7 | convolution fusion | flops 536870912 | bytes 6422528 | tf_op jit(solution)/shard_map/skc,dc->skd/dot_general | solution.py:71
  119.3 1.5 fusion.2
  120.8 0.8 convert_element_type.98
  121.6 1.3 copy.44
  123.6 50.1 %all-reduce.4.cloned.1.call-done = bf16[1,128,4,4,256]{4,1,3,2,0:T(8,128)(2,1)} async-done(((bf16[1,128,4,4,256]{4,1,3,2,0:T(8,128)(2,1)}), bf16[1,128,4,4,256]{4,1,3,2,0:T(8,128)(2,1)}) %all-reduce.4.cloned.1.call-update) | async-done | bytes 1048592
  173.7 2.3 constant_dynamic-slice_fusion
  176.1 1.6 convolution_convert_fusion.1
  177.7 0.8 copy.45
  178.6 2.0 convolution_convert_fusion
  180.6 0.8 copy.46
  181.4 18.8 %reduce-scatter.10.cloned.1.call-done = bf16[1,128,1,1,256]{4,1,3,2,0:T(8,128)(2,1)} async-done(((bf16[1,128,4,1,256]{4,1,3,2,0:T(8,128)(2,1)}), bf16[1,128,1,1,256]{4,1,3,2,0:T(8,128)(2,1)}) %reduce-scatter.10.cloned.1.call-update) | async-done | bytes 65552
  200.2 1.0 fusion.41
  201.3 41.0 %psum.22 = f32[1,128,1]{1,2,0:T(1,128)S(1)} all-reduce(f32[1,128,1]{1,2,0:T(1,128)S(1)} %bitcast.126), channel_id=1, replica_groups=mesh['section'=4,'dp'=2,'mp'=4] {'section','mp'}, use_global_device_ids=true, to_apply=%region_8.0 | all-reduce | flops 128 | bytes 1024 | tf_op jit(solution)/shard_map/psum | solution.py:85
  242.2 2.5 psum.23
  245.3 1.6 fusion.37
  (36 shorter events, 4.9 us)
Async XLA Ops:
  7.2 98.5 %all-gather.2.cloned.1.call-start = ((), (), s32[]{:S(2)}) async-start(), calls=%async_computation.1 | async-start | bytes 1114112 | tf_op jit(solution)/shard_map/all_gather | solution.py:65
  54.2 119.5 %all-reduce.4.cloned.1.call-start = ((), (), s32[]{:S(2)}) async-start(), calls=%async_computation.2 | async-start | bytes 2097152
  105.7 3.7 %copy-start.1 = (bf16[1,4096,512]{2,1,0:T(8,128)(2,1)S(1)}, bf16[1,4096,512]{2,1,0:T(8,128)(2,1)}, u32[]{:S(2)}) copy-start(bf16[1,4096,512]{2,1,0:T(8,128)(2,1)} %param.8) | copy-start | bytes 12582916
  105.7 4.0 %copy-start.2 = (bf16[1,128,4096]{2,1,0:T(8,128)(2,1)S(1)}, bf16[1,128,4096]{2,1,0:T(8,128)(2,1)}, u32[]{:S(2)}) copy-start(bf16[1,128,4096]{2,1,0:T(8,128)(2,1)} %all-gather.2.cloned.1.call-done) | copy-start | bytes 3145732
  110.8 4.5 %copy-start.4 = (bf16[1,128,512]{1,2,0:T(8,128)(2,1)}, bf16[1,128,512]{1,2,0:T(8,128)(2,1)S(1)}, u32[]{:S(2)}) copy-start(bf16[1,128,512]{1,2,0:T(8,128)(2,1)S(1)} %copy.37) | copy-start | bytes 393220
  112.3 3.1 %copy-start.7 = (f32[8,256]{1,0:T(8,128)}, f32[8,256]{1,0:T(8,128)S(1)}, u32[]{:S(2)}) copy-start(f32[8,256]{1,0:T(8,128)S(1)} %get-tuple-element.20) | copy-start | bytes 24580
  115.4 3.8 %copy-start = (bf16[1,4096,512]{2,1,0:T(8,128)(2,1)S(1)}, bf16[1,4096,512]{2,1,0:T(8,128)(2,1)}, u32[]{:S(2)}) copy-start(bf16[1,4096,512]{2,1,0:T(8,128)(2,1)} %param.9) | copy-start | bytes 12582916
  120.8 2.3 copy-start.6
  121.6 57.0 %copy-start.5 = (bf16[1,128,512]{1,2,0:T(8,128)(2,1)S(1)}, bf16[1,128,512]{1,2,0:T(8,128)(2,1)}, u32[]{:S(2)}) copy-start(bf16[1,128,512]{1,2,0:T(8,128)(2,1)} %copy-done.4) | copy-start | bytes 393220
  121.6 57.0 %copy-start.8 = (f32[8,256]{1,0:T(8,128)S(1)}, f32[8,256]{1,0:T(8,128)}, u32[]{:S(2)}) copy-start(f32[8,256]{1,0:T(8,128)} %copy-done.7) | copy-start | bytes 24580
  122.9 77.3 %reduce-scatter.10.cloned.1.call-start = ((), (), s32[]{:S(2)}) async-start(), calls=%async_computation.3 | async-start | bytes 327680
  177.7 22.5 %copy-start.3 = (bf16[1,128,256]{2,1,0:T(8,128)(2,1)S(1)}, bf16[1,128,256]{2,1,0:T(8,128)(2,1)}, u32[]{:S(2)}) copy-start(bf16[1,128,256]{2,1,0:T(8,128)(2,1)} %param.6) | copy-start | bytes 196612
Sparse Core Ops, SparseCore 0:
  54.4 51.2 all-gather.1
  123.1 50.6 all-reduce.3
  176.7 23.4 reduce-scatter.9
where the time goes:
time: 254 us; the launch traced here: 253 us
  waiting for transfers between devices  118 us (46%)
  blocking collectives  87.1 us (34%)
  matrix products  17.6 us (7%)
  between operations  14 us (6%)
  local copies, waits for them, and re-layouts  10.6 us (4%)
  other arithmetic  5.72 us (2%)
    unnamed x5, waiting for transfers between devices  69 us
    all_gather x1, waiting for transfers between devices, per_device(): memory = lax.all_gather(own_memory, ('section', 'mp'), axis=2, tiled=True)  49.2 us
    psum x1, blocking collectives, per_device(): lax.psum(jnp.sum(widened * widened, axis=-1, keepdims=True), ('section',...  43.7 us
    psum x1, blocking collectives, per_device(): lax.psum(jnp.sum(scaled * normed, axis=-1, keepdims=True), ('section', 'm...  41 us
    unnamed x24, local copies, waits for them, and re-layouts  7.49 us
  transfers between devices with their start and end apart: 3, of which 3 were waited for; matrix products, arithmetic and copies ran while one was open for 3% of the time, Pallas kernels for 0%

commit v1 on v0

--- a/solution.py
+++ b/solution.py
@@ -58,7 +58,9 @@
     first_column = lax.axis_index(("section", "mp")) * own_columns
     gain_own = lax.dynamic_slice_in_dim(enc_gain, first_column, own_columns, 0)
     widened = enc_hidden.astype(jnp.float32)
-    squares = lax.psum(jnp.sum(widened * widened, axis=-1, keepdims=True), ("section", "mp"))
+    squares = lax.psum(
+        lax.psum(jnp.sum(widened * widened, axis=-1, keepdims=True), "mp"), "section"
+    )
     inverse = lax.rsqrt(squares / width + epsilon)
     normed = widened * inverse
     own_memory = (normed * gain_own).astype(jnp.bfloat16)

time: 254 us -> 234 us (0.921)
  blocking collectives: 87.1 us -> 66.8 us
    psum x1 -> x2, blocking collectives: 43.7 us -> 23.4 us  [the longest x1 13.5 us: per_device(): lax.psum(jnp.sum(widened * widened, axis=-1, keepdims=True), 'mp')]
where the time goes in v1:
time: 234 us; the launch traced here: 233 us
  waiting for transfers between devices  118 us (50%)
  blocking collectives  66.8 us (29%)
  matrix products  17.6 us (8%)
  between operations  13.9 us (6%)
  local copies, waits for them, and re-layouts  10.6 us (5%)
  other arithmetic  5.72 us (2%)
    unnamed x5, waiting for transfers between devices  69 us
    all_gather x1, waiting for transfers between devices, per_device(): memory = lax.all_gather(own_memory, ('section', 'mp'), axis=2, tiled=True)  49.3 us
    psum x1, blocking collectives, per_device(): lax.psum(jnp.sum(scaled * normed, axis=-1, keepdims=True), ('section', 'm...  41 us
    psum x1, blocking collectives, per_device(): lax.psum(jnp.sum(widened * widened, axis=-1, keepdims=True), 'mp')  13.5 us
    psum x1, blocking collectives, per_device(): lax.psum(lax.psum(jnp.sum(widened * widened, axis=-1, keepdims=True), 'mp...  9.89 us
    unnamed x24, local copies, waits for them, and re-layouts  7.49 us
  transfers between devices with their start and end apart: 3, of which 3 were waited for; matrix products, arithmetic and copies ran while one was open for 3% of the time, Pallas kernels for 0%

profile of v1, /device:TPU:0, one launch (start us, length us, event | category | flops | bytes accessed | tf_op | source)
XLA Modules:
  0.0 233.2 jit_solution(10809075548189412303)
XLA Ops:
  7.2 0.9 fusion.40
  8.2 13.5 %psum.28 = f32[1,128,1]{1,2,0:T(1,128)S(1)} all-reduce(f32[1,128,1]{1,2,0:T(1,128)S(1)} %bitcast.127), channel_id=1, replica_groups=mesh['section'=4,'dp'=2,'mp'=4] {'mp'}, use_global_device_ids=true, to_apply=%region_1.0 | all-reduce | flops 128 | bytes 1024 | tf_op jit(solution)/shard_map/psum | solution.py:62
  21.6 9.9 %psum.29 = f32[1,128,1]{1,2,0:T(1,128)S(1)} all-reduce(f32[1,128,1]{1,2,0:T(1,128)S(1)} %psum.28), channel_id=1, replica_groups=mesh['section'=4,'dp'=2,'mp'=4] {'section'}, use_global_device_ids=true, to_apply=%region_2.0 | all-reduce | flops 128 | bytes 1024 | tf_op jit(solution)/shard_map/psum | solution.py:61
  32.3 1.6 fusion.38
  33.9 1.1 copy.38
  35.0 1.1 copy.40
  36.1 49.3 %all-gather.2.cloned.1.call-done = bf16[1,128,4096]{2,1,0:T(8,128)(2,1)} async-done(((bf16[1,128,256]{2,1,0:T(8,128)(2,1)}), bf16[1,128,4096]{2,1,0:T(8,128)(2,1)}) %all-gather.2.cloned.1.call-update) | async-done | bytes 1048592 | tf_op jit(solution)/shard_map/all_gather | solution.py:67
  85.5 3.4 %fusion.20 = bf16[128,512]{1,0:T(8,128)(2,1)S(1)} fusion(bf16[1,4096,512]{2,1,0:T(8,128)(2,1)} %param.9, bf16[1,128,4096]{2,1,0:T(8,128)(2,1)} %all-gather.2.cloned.1.call-done), kind=kOutput, calls=%fused_computation.23 | convolution fusion | flops 536936448 | bytes 5373952 | tf_op jit(solution)/shard_map/dot_general | solution.py:70
  90.6 1.5 fusion.49
  93.1 2.0 convolution_convert_fusion.3
  95.2 3.8 %fusion.6 = f32[128,4096]{1,0:T(8,128)S(1)} fusion(bf16[128,512]{0,1:T(8,128)(2,1)S(1)} %bitcast.121, bf16[1,4096,512]{2,1,0:T(8,128)(2,1)} %param.8), kind=kOutput, calls=%fused_computation.7 | convolution fusion | flops 536870912 | bytes 6422528 | tf_op jit(solution)/shard_map/skc,dc->skd/dot_general | solution.py:73
  99.0 1.5 fusion.2
  101.4 1.3 copy.44
  103.4 50.2 %all-reduce.4.cloned.1.call-done = bf16[1,128,4,4,256]{4,1,3,2,0:T(8,128)(2,1)} async-done(((bf16[1,128,4,4,256]{4,1,3,2,0:T(8,128)(2,1)}), bf16[1,128,4,4,256]{4,1,3,2,0:T(8,128)(2,1)}) %all-reduce.4.cloned.1.call-update) | async-done | bytes 1048592
  153.5 2.3 %constant_dynamic-slice_fusion = bf16[1,128,4,1,256]{4,1,3,2,0:T(8,128)(2,1)} fusion(bf16[1,128,4,4,256]{4,1,3,2,0:T(8,128)(2,1)} %all-reduce.4.cloned.1.call-done, u32[]{:T(128)} %bitcast.56), kind=kLoop, calls=%fused_computation.50 | loop fusion | bytes 524292
  155.9 1.6 convolution_convert_fusion.1
  157.5 0.8 copy.45
  158.3 2.0 convolution_convert_fusion
  160.3 0.9 copy.46
  161.2 18.8 %reduce-scatter.10.cloned.1.call-done = bf16[1,128,1,1,256]{4,1,3,2,0:T(8,128)(2,1)} async-done(((bf16[1,128,4,1,256]{4,1,3,2,0:T(8,128)(2,1)}), bf16[1,128,1,1,256]{4,1,3,2,0:T(8,128)(2,1)}) %reduce-scatter.10.cloned.1.call-update) | async-done | bytes 65552
  180.0 1.0 fusion.41
  181.0 41.0 %psum.30 = f32[1,128,1]{1,2,0:T(1,128)S(1)} all-reduce(f32[1,128,1]{1,2,0:T(1,128)S(1)} %bitcast.126), channel_id=1, replica_groups=mesh['section'=4,'dp'=2,'mp'=4] {'section','mp'}, use_global_device_ids=true, to_apply=%region_9.0 | all-reduce | flops 128 | bytes 1024 | tf_op jit(solution)/shard_map/psum | solution.py:87
  222.0 2.5 %psum.31 = f32[256]{0:T(256)S(1)} all-reduce(f32[256]{0:T(256)S(1)} %get-tuple-element.16), channel_id=1, replica_groups=mesh['section'=4,'dp'=2,'mp'=4] {'dp'}, use_global_device_ids=true, to_apply=%region_11.0 | all-reduce | flops 256 | bytes 2048 | tf_op jit(solution)/shard_map/psum | solution.py:88
  225.0 1.6 fusion.37
  (37 shorter events, 5.7 us)
Async XLA Ops:
  7.2 78.3 %all-gather.2.cloned.1.call-start = ((), (), s32[]{:S(2)}) async-start(), calls=%async_computation.1 | async-start | bytes 1114112 | tf_op jit(solution)/shard_map/all_gather | solution.py:67
  33.9 119.6 %all-reduce.4.cloned.1.call-start = ((), (), s32[]{:S(2)}) async-start(), calls=%async_computation.2 | async-start | bytes 2097152
  85.5 3.7 %copy-start.1 = (bf16[1,4096,512]{2,1,0:T(8,128)(2,1)S(1)}, bf16[1,4096,512]{2,1,0:T(8,128)(2,1)}, u32[]{:S(2)}) copy-start(bf16[1,4096,512]{2,1,0:T(8,128)(2,1)} %param.8) | copy-start | bytes 12582916
  85.5 4.0 %copy-start.2 = (bf16[1,128,4096]{2,1,0:T(8,128)(2,1)S(1)}, bf16[1,128,4096]{2,1,0:T(8,128)(2,1)}, u32[]{:S(2)}) copy-start(bf16[1,128,4096]{2,1,0:T(8,128)(2,1)} %all-gather.2.cloned.1.call-done) | copy-start | bytes 3145732
  90.6 4.5 %copy-start.4 = (bf16[1,128,512]{1,2,0:T(8,128)(2,1)}, bf16[1,128,512]{1,2,0:T(8,128)(2,1)S(1)}, u32[]{:S(2)}) copy-start(bf16[1,128,512]{1,2,0:T(8,128)(2,1)S(1)} %copy.37) | copy-start | bytes 393220
  92.1 3.1 %copy-start.7 = (f32[8,256]{1,0:T(8,128)}, f32[8,256]{1,0:T(8,128)S(1)}, u32[]{:S(2)}) copy-start(f32[8,256]{1,0:T(8,128)S(1)} %get-tuple-element.20) | copy-start | bytes 24580
  95.2 3.8 %copy-start = (bf16[1,4096,512]{2,1,0:T(8,128)(2,1)S(1)}, bf16[1,4096,512]{2,1,0:T(8,128)(2,1)}, u32[]{:S(2)}) copy-start(bf16[1,4096,512]{2,1,0:T(8,128)(2,1)} %param.9) | copy-start | bytes 12582916
  100.5 2.2 copy-start.6
  101.3 57.0 %copy-start.5 = (bf16[1,128,512]{1,2,0:T(8,128)(2,1)S(1)}, bf16[1,128,512]{1,2,0:T(8,128)(2,1)}, u32[]{:S(2)}) copy-start(bf16[1,128,512]{1,2,0:T(8,128)(2,1)} %copy-done.4) | copy-start | bytes 393220
  101.3 57.0 %copy-start.8 = (f32[8,256]{1,0:T(8,128)S(1)}, f32[8,256]{1,0:T(8,128)}, u32[]{:S(2)}) copy-start(f32[8,256]{1,0:T(8,128)} %copy-done.7) | copy-start | bytes 24580
  102.7 77.3 %reduce-scatter.10.cloned.1.call-start = ((), (), s32[]{:S(2)}) async-start(), calls=%async_computation.3 | async-start | bytes 327680
  157.5 22.5 %copy-start.3 = (bf16[1,128,256]{2,1,0:T(8,128)(2,1)S(1)}, bf16[1,128,256]{2,1,0:T(8,128)(2,1)}, u32[]{:S(2)}) copy-start(bf16[1,128,256]{2,1,0:T(8,128)(2,1)} %param.6) | copy-start | bytes 196612
Sparse Core Ops, SparseCore 0:
  34.0 51.4 all-gather.1
  102.8 50.6 all-reduce.3
  156.5 23.4 reduce-scatter.9
